TPU v7x, 256 devices: a whole 4x4x8 slice. The times are simulated.
256 devices in a mesh: dp: 128 (over z, x, y), sub: 2 (over core).
Axes of the slice: x: 4, y: 4, z: 8, core: 2. Of those that a mesh axis runs over, the one named last changes fastest.
Arguments:
- queries: bfloat16 [49152, 4096], P('dp', 'sub'), may hold values from -32 to 32
- passages: bfloat16 [49152, 4096], P('dp', 'sub'), may hold values from -8 to 8
- positive: int32 [128, 384], P('dp'), may hold values from 0 to 383, each once within a row
- pair_on: int32 [128, 3], replicated, may hold values from 0 to 1, as said below
Outputs:
- loss: float32 [1], replicated
- query_grad: float32 [49152, 4096], P('dp', 'sub')
- passage_grad: float32 [49152, 4096], P('dp', 'sub')
Inputs may be any that keep to these rules, and one draw needn't show every extreme that they name: pair_on[s, k] equals pair_on[s xor 2 ** (log2(128) - 3 + k), k]; shards 0 and 2 ** (log2(128) - 3) - 1 pair at every level.
All inputs are finite; a program needn't handle non-finite values.
Results may differ from a plain program's by a relative error of at most 0.0016.
Values may be sent and summed in bfloat16 or wider, within the bound.
A program may use at most 128 MiB of HBM per device.

v0:
```python
import math

import jax
import jax.numpy as jnp
from jax import lax
from jax.sharding import PartitionSpec as P

D = 4096


def swapped(block, axis, bit):
    count = lax.axis_size(axis)
    route = []
    for low in range(count):
        high = low | 1 << bit
        if high != low and high < count:
            route += [(low, high), (high, low)]
    return lax.ppermute(block, axis, route)


def tile_logits(left, right):
    return lax.dot_general(
        left, right, (((1,), (1,)), ((), ())), preferred_element_type=jnp.float32
    ) / math.sqrt(D)


def transposed_product(grad, block):
    return lax.dot_general(
        grad, block, (((0,), (0,)), ((), ())), preferred_element_type=jnp.float32
    )


def lse_axis(values, axis):
    return jax.scipy.special.logsumexp(values, axis=axis)


def local(queries, passages, positive, pair_on):
    rows, width = queries.shape
    levels = pair_on.shape[1]
    me = lax.axis_index("dp")
    depth = lax.axis_size("dp").bit_length() - 1
    level_bits = []
    actives = []
    far_blocks = []
    partial_tiles = [tile_logits(queries, passages)]
    for level in range(levels):
        bit = depth - levels + level
        active = pair_on[me, level] > 0
        received = swapped(jnp.stack([queries, passages]), "dp", bit)
        far_q = received[0]
        far_p = received[1]
        pair_tile = lax.cond(
            active,
            lambda: tile_logits(queries, far_p),
            lambda: jnp.zeros((rows, rows), jnp.float32),
        )
        partial_tiles.append(pair_tile)
        level_bits.append(bit)
        actives.append(active)
        far_blocks.append((far_q, far_p))
    summed = lax.psum(jnp.stack(partial_tiles), "sub")
    own = summed[0]
    columns = jnp.arange(rows, dtype=jnp.int32)
    onehot = (positive[0][:, None] == columns[None, :]).astype(jnp.float32)
    row_lse = lse_axis(own, 1)
    col_lse = lse_axis(own, 0)
    for level in range(levels):
        tile = summed[1 + level]
        active = actives[level]
        row_lse = jnp.where(active, jnp.logaddexp(row_lse, lse_axis(tile, 1)), row_lse)
        outgoing = jnp.where(active, lse_axis(tile, 0), -jnp.inf)
        incoming = swapped(outgoing, "dp", level_bits[level])
        col_lse = jnp.where(active, jnp.logaddexp(col_lse, incoming), col_lse)
    grad_own = (
        jnp.exp(own - row_lse[:, None]) + jnp.exp(own - col_lse[None, :]) - 2.0 * onehot
    ).astype(jnp.bfloat16)
    query_grad = jnp.dot(grad_own, passages, preferred_element_type=jnp.float32)
    passage_grad = transposed_product(grad_own, queries)
    for level in range(levels):
        bit = level_bits[level]
        active = actives[level]
        far_q, far_p = far_blocks[level]
        tile = summed[1 + level]
        far_cols = swapped(col_lse, "dp", bit)
        g_tile = jnp.exp(tile - row_lse[:, None]) + jnp.exp(tile - far_cols[None, :])
        g_tile = jnp.where(active, g_tile, 0.0).astype(jnp.bfloat16)
        near_term = lax.cond(
            active,
            lambda: jnp.dot(g_tile, far_p, preferred_element_type=jnp.float32),
            lambda: jnp.zeros((rows, width), jnp.float32),
        )
        query_grad = query_grad + near_term
        back = lax.cond(
            active,
            lambda: transposed_product(g_tile, queries),
            lambda: jnp.zeros((rows, width), jnp.float32),
        )
        returned = swapped(back, "dp", bit)
        passage_grad = passage_grad + jnp.where(active, returned, 0.0)
    local_total = jnp.sum(row_lse) + jnp.sum(col_lse) - 2.0 * jnp.sum(own * onehot)
    total = lax.psum(local_total, "dp")
    loss = jnp.reshape(total / (2.0 * rows * lax.axis_size("dp")), (1,))
    return (loss, query_grad, passage_grad)


def solution(mesh):
    placed = (P("dp", "sub"), P("dp", "sub"), P("dp", None), P())
    return jax.shard_map(
        local,
        mesh=mesh,
        in_specs=placed,
        out_specs=(P(), P("dp", "sub"), P("dp", "sub")),
        check_vma=False,
    )
```

profile of v0, /device:TPU:32, one launch (start us, length us, event | category | flops | bytes accessed | tf_op | source)
XLA Modules:
  0.0 979.4 jit_solution(10727603382917345739)
XLA Ops:
  7.2 4.0 pad_maximum_fusion
  11.2 6.3 collective-permute-start.2
  24.4 130.9 %collective-permute-done.2 = bf16[2,384,2048]{2,1,0:T(8,128)(2,1)} collective-permute-done((bf16[2,384,2048]{2,1,0:T(8,128)(2,1)}, bf16[2,384,2048]{2,1,0:T(8,128)(2,1)}, u32[]{:S(2)}, u32[]{:S(2)}) %collective-permute-start.2) | collective-permute-done | bytes 3145760 | tf_op jit(solution)/shard_map/ppermute | solution.py:18
  155.3 2.7 slice_bitcast_fusion
  158.1 130.1 %collective-permute-done.1 = bf16[2,384,2048]{2,1,0:T(8,128)(2,1)} collective-permute-done((bf16[2,384,2048]{2,1,0:T(8,128)(2,1)}, bf16[2,384,2048]{2,1,0:T(8,128)(2,1)}, u32[]{:S(2)}, u32[]{:S(2)}) %collective-permute-start.1) | collective-permute-done | bytes 3145760 | tf_op jit(solution)/shard_map/ppermute | solution.py:18
  288.1 2.8 slice_bitcast_fusion.1
  292.4 3.3 conditional.11
  292.4 3.3 fusion.2
  295.7 3.2 conditional.10
  295.7 3.2 fusion.1
  300.7 3.2 pad_maximum_fusion.1
  304.6 31.5 %all-reduce.2.cloned.1.call-done = f32[4,384,384]{2,1,0:T(8,128)} async-done(((f32[4,384,384]{2,1,0:T(8,128)}), f32[4,384,384]{2,1,0:T(8,128)}) %all-reduce.2.cloned.1.call-update) | async-done | bytes 2359312 | tf_op jit(solution)/shard_map/psum | solution.py:61
  336.1 2.0 slice_reduce_fusion.6
  340.2 4.8 collective-permute-start.5
  356.1 5.0 collective-permute-done.8
  362.6 3.7 conditional.17
  362.6 3.7 fusion.52
  368.0 3.6 conditional.16
  368.0 3.6 fusion.51
  372.2 2.7 conditional.15
  372.2 2.7 fusion.50
  377.5 559.5 %psum.15 = f32[]{:T(128)} all-reduce(f32[]{:T(128)S(6)} %sub.180), channel_id=1, replica_groups=mesh['dp'=128,'sub'=2] {'dp'}, use_global_device_ids=true, to_apply=%region_26.27 | all-reduce | flops 1 | bytes 8 | tf_op jit(solution)/shard_map/psum | solution.py:101
  937.7 4.4 fusion.43
  942.1 3.9 fusion.41
  945.9 4.3 conditional.14
  945.9 4.3 fusion.49
  950.2 3.6 conditional.13
  950.2 3.6 fusion.48
  953.8 2.6 conditional.12
  953.8 2.6 fusion.47
  956.4 8.1 add_add_fusion
  964.6 6.8 select_add_fusion
  (52 shorter events, 28.3 us)
Async XLA Ops:
  7.2 328.9 %all-reduce.2.cloned.1.call-start = ((), (), s32[]{:S(2)}) async-start(), calls=%async_computation | async-start | bytes 4718592 | tf_op jit(solution)/shard_map/psum | solution.py:61
  7.2 12.8 %copy-start.6 = (s32[128,3]{0,1:T(4,128)S(1)}, s32[128,3]{0,1:T(4,128)}, u32[]{:S(2)}) copy-start(s32[128,3]{0,1:T(4,128)} %param.25) | copy-start | bytes 4612
  7.2 15.4 %copy-start = (bf16[384,2048]{1,0:T(8,128)(2,1)S(1)}, bf16[384,2048]{1,0:T(8,128)(2,1)}, u32[]{:S(2)}) copy-start(bf16[384,2048]{1,0:T(8,128)(2,1)} %param.22) | copy-start | bytes 4718596
  7.2 15.4 %copy-start.4 = (bf16[384,2048]{1,0:T(8,128)(2,1)S(1)}, bf16[384,2048]{1,0:T(8,128)(2,1)}, u32[]{:S(2)}) copy-start(bf16[384,2048]{1,0:T(8,128)(2,1)} %param.23) | copy-start | bytes 4718596
  11.2 144.1 %collective-permute-start.2 = (bf16[2,384,2048]{2,1,0:T(8,128)(2,1)}, bf16[2,384,2048]{2,1,0:T(8,128)(2,1)}, u32[]{:S(2)}, u32[]{:S(2)}) collective-permute-start(bf16[2,384,2048]{2,1,0:T(8,128)(2,1)} %pad_maximum_fusion), channel_id=1, source_target_pairs={{0,128},{128,0},{2,130},{130,2},{4,132},{132,4},{6,134},{134,6},{8... | collective-permute-start | bytes 9437192 | tf_op jit(solution)/shard_map/ppermute | solution.py:18
  17.5 270.6 %collective-permute-start.1 = (bf16[2,384,2048]{2,1,0:T(8,128)(2,1)}, bf16[2,384,2048]{2,1,0:T(8,128)(2,1)}, u32[]{:S(2)}, u32[]{:S(2)}) collective-permute-start(bf16[2,384,2048]{2,1,0:T(8,128)(2,1)} %pad_maximum_fusion), channel_id=1, source_target_pairs={{0,64},{64,0},{2,66},{66,2},{4,68},{68,4},{6,70},{70,6},{8,72},{72... | collective-permute-start | bytes 9437192 | tf_op jit(solution)/shard_map/ppermute | solution.py:18
  19.0 271.9 %collective-permute-start = (bf16[2,384,2048]{2,1,0:T(8,128)(2,1)}, bf16[2,384,2048]{2,1,0:T(8,128)(2,1)}, u32[]{:S(2)}, u32[]{:S(2)}) collective-permute-start(bf16[2,384,2048]{2,1,0:T(8,128)(2,1)} %pad_maximum_fusion), channel_id=1, source_target_pairs={{0,32},{32,0},{2,34},{34,2},{4,36},{36,4},{6,38},{38,6},{8,40},{40... | collective-permute-start | bytes 9437192 | tf_op jit(solution)/shard_map/ppermute | solution.py:18
  303.9 0.7 copy-start.5
  336.1 2.4 copy-start.1
  340.2 7.5 collective-permute-start.5
  345.1 4.5 collective-permute-start.4
  345.8 3.7 collective-permute-start.3
  350.3 5.8 collective-permute-start.6
  351.7 4.5 collective-permute-start.7
  353.7 7.5 collective-permute-start.8
  366.3 598.2 %collective-permute-start.11 = (f32[384,2048]{1,0:T(8,128)}, f32[384,2048]{1,0:T(8,128)}, u32[]{:S(2)}, u32[]{:S(2)}) collective-permute-start(f32[384,2048]{1,0:T(8,128)} %get-tuple-element.130), channel_id=1, source_target_pairs={{0,128},{128,0},{2,130},{130,2},{4,132},{132,4},{6,134},{134,6},{8... | collective-permute-start | bytes 9437192 | tf_op jit(solution)/shard_map/ppermute | solution.py:18
  371.6 592.9 %collective-permute-start.10 = (f32[384,2048]{1,0:T(8,128)}, f32[384,2048]{1,0:T(8,128)}, u32[]{:S(2)}, u32[]{:S(2)}) collective-permute-start(f32[384,2048]{1,0:T(8,128)} %get-tuple-element.129), channel_id=1, source_target_pairs={{0,64},{64,0},{2,66},{66,2},{4,68},{68,4},{6,70},{70,6},{8,72},{72... | collective-permute-start | bytes 9437192 | tf_op jit(solution)/shard_map/ppermute | solution.py:18
  374.9 589.6 %collective-permute-start.9 = (f32[384,2048]{1,0:T(8,128)}, f32[384,2048]{1,0:T(8,128)}, u32[]{:S(2)}, u32[]{:S(2)}) collective-permute-start(f32[384,2048]{1,0:T(8,128)} %get-tuple-element.128), channel_id=1, source_target_pairs={{0,32},{32,0},{2,34},{34,2},{4,36},{36,4},{6,38},{38,6},{8,40},{40... | collective-permute-start | bytes 9437192 | tf_op jit(solution)/shard_map/ppermute | solution.py:18
  945.9 4.3 copy-start.3
  956.4 8.1 copy-start.2
Sparse Core Ops, SparseCore 0:
  304.0 32.0 all-reduce.1
where the time goes:
time: 980 us; the launch traced here: 979 us
  blocking collectives  560 us (57%)
  waiting for transfers between devices  300 us (31%)
  matrix products  38.9 us (4%)
  other arithmetic  28.7 us (3%)
  starting transfers between devices  23.9 us (2%)
  between operations  19.8 us (2%)
    psum x1, blocking collectives, local(): total = lax.psum(local_total, 'dp')  560 us
    ppermute x12, waiting for transfers between devices, swapped(): return lax.ppermute(block, axis, route)  268 us
    psum x1, waiting for transfers between devices, local(): summed = lax.psum(jnp.stack(partial_tiles), 'sub')  31.5 us
    ppermute x12, starting transfers between devices, swapped(): return lax.ppermute(block, axis, route)  23.8 us
  transfers between devices with their start and end apart: 13, of which 7 were waited for; matrix products, arithmetic and copies ran while one was open for 4% of the time, Pallas kernels for 0%

commit v1 on v0

v1 whole, which is shorter than its diff:
```python
import functools
import math

import jax
import jax.numpy as jnp
from jax import lax
from jax.experimental import pallas as pl
from jax.experimental.pallas import tpu as pltpu
from jax.sharding import PartitionSpec as P

MESH = pl.DeviceIdType.MESH
NZ = 8
LEVELS = 3
CHUNKS = 8
F32 = jnp.float32
BF16 = jnp.bfloat16

P_UP0, P_UP1, P_UP2, P_DN0, P_DN1, P_OWN = range(6)
Q_UP0, Q_UP1, Q_DN0, Q_DN1, Q_DN2, Q_OWN = range(6)
T_OWN, T_U0, T_L0, T_X = 0, 1, 4, 7


def dot_nt(a, b):
    return lax.dot_general(a, b, (((1,), (1,)), ((), ())), preferred_element_type=F32)


def dot_nn(a, b):
    return jnp.dot(a, b, preferred_element_type=F32)


def to_lanes(column):
    rows = column.shape[0]
    return jnp.transpose(jnp.broadcast_to(column, (rows, 128)))[0:1, :]


def to_column(lanes):
    rows = lanes.shape[1]
    return jnp.transpose(jnp.broadcast_to(lanes, (128, rows)))[:, 0:1]


def lse_rows(tile):
    top = jnp.max(tile, axis=1, keepdims=True)
    return top + jnp.log(jnp.sum(jnp.exp(tile - top), axis=1, keepdims=True))


def lse_cols(tile):
    top = jnp.max(tile, axis=0, keepdims=True)
    return top + jnp.log(jnp.sum(jnp.exp(tile - top), axis=0, keepdims=True))


def kernel(
    nx, ny, scale, count,
    q_hbm, p_hbm, pos_ref, pair_ref,
    loss_ref, dq_hbm, dp_hbm,
    pb, qb, cin, cs, cm, part, got, dqv, dpv,
    g_own, g_own_t, g_up, g_up0_t, g_low, g_x,
    ms1, mr1, ms2, mr2, lz, lx, ly,
    own_sem, out_sem,
    p_send_up, p_send_dn, p_recv,
    q_send_up, q_send_dn, q_recv,
    c_send, c_recv,
    t_send, t_recv,
    m1_send, m1_recv, m2_send, m2_recv,
    z_send, z_recv, x_send, x_recv, y_send, y_recv,
):
    rows = pb.shape[2]
    width = pb.shape[3]
    per_z = nx * ny
    dp = lax.axis_index("dp")
    sub = lax.axis_index("sub")
    z = dp // per_z
    xy = dp % per_z
    x = xy // ny
    y = xy % ny
    role = z % 4
    second = role // 2
    sign = 1 - 2 * second
    outer = (role % 3) == 0
    inner = jnp.logical_not(outer)

    def at_z(other):
        return (((other + 2 * NZ) % NZ) * per_z + xy, sub)

    up = at_z(z + sign)
    down = at_z(z - sign)
    twin = (dp, 1 - sub)

    def partner_z(level):
        step = 1 << level
        return z + step - 2 * step * ((z // step) % 2)

    partners = [at_z(partner_z(level)) for level in range(LEVELS)]
    far2 = at_z(z - 2 * sign)

    def remote(src, dst, send, recv, device):
        return pltpu.make_async_remote_copy(
            src_ref=src, dst_ref=dst, send_sem=send, recv_sem=recv,
            device_id=device, device_id_type=MESH,
        )

    def p_up(i, src, dst, k):
        return remote(pb.at[src, k], pb.at[dst, k], p_send_up.at[i, k], p_recv.at[dst, k], up)

    def p_dn(i, src, dst, k):
        return remote(pb.at[src, k], pb.at[dst, k], p_send_dn.at[i, k], p_recv.at[dst, k], down)

    def q_up(i, src, dst, k):
        return remote(qb.at[src, k], qb.at[dst, k], q_send_up.at[i, k], q_recv.at[dst, k], up)

    def q_dn(i, src, dst, k):
        return remote(qb.at[src, k], qb.at[dst, k], q_send_dn.at[i, k], q_recv.at[dst, k], down)

    def c_up(k):
        return remote(cs.at[k], cin.at[k], c_send.at[0, k], c_recv.at[k], up)

    def c_dn(k):
        return remote(cm.at[k], cin.at[k], c_send.at[1, k], c_recv.at[k], down)

    def p_wait(slot, k):
        remote(pb.at[slot, k], pb.at[slot, k], p_send_up.at[0, k], p_recv.at[slot, k], up).wait_recv()

    def q_wait(slot, k):
        remote(qb.at[slot, k], qb.at[slot, k], q_send_up.at[0, k], q_recv.at[slot, k], up).wait_recv()

    def tile_copy(i):
        return remote(part.at[i], got.at[i], t_send.at[i], t_recv.at[i], twin)

    def finish_tile(i):
        tile_copy(i).wait_recv()
        got[i] = (got[i] + part[i]) * scale

    def m1_copy(level):
        return remote(ms1.at[level], mr1.at[level], m1_send.at[level], m1_recv.at[level], partners[level])

    def m2_copy(i):
        device = partners[i] if i < LEVELS else far2
        return remote(ms2, mr2.at[i], m2_send.at[i], m2_recv.at[i], device)

    def z_copy(d):
        return remote(lz.at[z], lz.at[z], z_send.at[d], z_recv.at[z], at_z(z + d))

    def z_wait(d):
        other = (z + d) % NZ
        remote(lz.at[other], lz.at[other], z_send.at[d], z_recv.at[other], at_z(z + d)).wait_recv()

    def x_device(d):
        return (z * per_z + ((x + d) % nx) * ny + y, sub)

    def x_copy(d):
        return remote(lx.at[x], lx.at[x], x_send.at[d], x_recv.at[x], x_device(d))

    def x_wait(d):
        other = (x + d) % nx
        remote(lx.at[other], lx.at[other], x_send.at[d], x_recv.at[other], x_device(d)).wait_recv()

    def y_device(d):
        return (z * per_z + x * ny + (y + d) % ny, sub)

    def y_copy(d):
        return remote(ly.at[y], ly.at[y], y_send.at[d], y_recv.at[y], y_device(d))

    def y_wait(d):
        other = (y + d) % ny
        remote(ly.at[other], ly.at[other], y_send.at[d], y_recv.at[other], y_device(d)).wait_recv()

    def load_p(k):
        return pltpu.make_async_copy(
            p_hbm.at[:, pl.ds(pl.multiple_of(k * width, width), width)], pb.at[P_OWN, k], own_sem.at[0, k]
        )

    def load_q(k):
        return pltpu.make_async_copy(
            q_hbm.at[:, pl.ds(pl.multiple_of(k * width, width), width)], qb.at[Q_OWN, k], own_sem.at[1, k]
        )

    def store_dq(k):
        return pltpu.make_async_copy(
            dqv.at[k], dq_hbm.at[:, pl.ds(pl.multiple_of(k * width, width), width)], out_sem.at[0, k]
        )

    def store_dp(k):
        return pltpu.make_async_copy(
            dpv.at[k], dp_hbm.at[:, pl.ds(pl.multiple_of(k * width, width), width)], out_sem.at[1, k]
        )

    def each_chunk(body):
        def step(k, carry):
            body(k)
            return carry

        lax.fori_loop(0, CHUNKS, step, 0)

    def add_tile(i, k, left, right):
        @pl.when(k == 0)
        def _():
            part[i] = dot_nt(left, right)

        @pl.when(k > 0)
        def _():
            part[i] = part[i] + dot_nt(left, right)

    @each_chunk
    def _(k):
        load_p(k).start()

    @each_chunk
    def _(k):
        load_q(k).start()

    barrier = pltpu.get_barrier_semaphore()
    greeted = [twin]
    greeted += [at_z(z + d) for d in range(1, NZ)]
    greeted += [x_device(d) for d in range(1, nx)]
    greeted += [y_device(d) for d in range(1, ny)]
    for device in greeted:
        pl.semaphore_signal(barrier, inc=1, device_id=device, device_id_type=MESH)
    pl.semaphore_wait(barrier, len(greeted))

    @each_chunk
    def _(k):
        load_p(k).wait()

        @pl.when(outer)
        def _():
            p_up(0, P_OWN, P_DN0, k).start()

        @pl.when(inner)
        def _():
            p_up(0, P_OWN, P_UP0, k).start()
            p_dn(0, P_OWN, P_UP0, k).start()

    @each_chunk
    def _(k):
        load_q(k).wait()

        @pl.when(outer)
        def _():
            q_dn(0, Q_OWN, Q_DN2, k).start()

    @each_chunk
    def _(k):
        add_tile(T_OWN, k, pb[P_OWN, k], qb[Q_OWN, k])

    tile_copy(T_OWN).start()

    near = jnp.where(outer, P_UP0, P_DN0)

    @each_chunk
    def _(k):
        @pl.when(inner)
        def _():
            p_wait(P_UP0, k)
            p_dn(1, P_UP0, P_UP1, k).start()

        p_wait(near, k)

        @pl.when(inner)
        def _():
            p_up(1, P_DN0, P_UP1, k).start()

        add_tile(T_U0, k, qb[Q_OWN, k], pb[near, k])

    tile_copy(T_U0).start()

    @each_chunk
    def _(k):
        p_wait(P_UP1, k)

        @pl.when(outer)
        def _():
            p_dn(0, P_UP1, P_DN0, k).start()

        @pl.when(inner)
        def _():
            p_dn(2, P_UP1, P_UP2, k).start()

        add_tile(T_U0 + 1, k, qb[Q_OWN, k], pb[P_UP1, k])

        @pl.when(outer)
        def _():
            p_wait(P_DN0, k)
            p_up(1, P_DN0, P_DN1, k).start()

    tile_copy(T_U0 + 1).start()

    @each_chunk
    def _(k):
        @pl.when(outer)
        def _():
            q_wait(Q_DN2, k)
            q_up(0, Q_DN2, Q_DN2, k).start()

        @pl.when(inner)
        def _():
            q_up(0, Q_OWN, Q_UP0, k).start()

    @each_chunk
    def _(k):
        @pl.when(outer)
        def _():
            p_wait(P_UP2, k)
            p_dn(1, P_UP2, P_DN1, k).start()

        p_wait(P_DN1, k)
        add_tile(T_U0 + 2, k, qb[Q_OWN, k], pb[P_DN1, k])

        @pl.when(inner)
        def _():
            q_wait(Q_DN2, k)
            add_tile(T_X, k, pb[P_UP1, k], qb[Q_DN2, k])

    tile_copy(T_U0 + 2).start()

    @pl.when(inner)
    def _():
        tile_copy(T_X).start()

    def q_first(k):
        @pl.when(outer)
        def _():
            q_up(1, Q_OWN, Q_DN0, k).start()

        @pl.when(inner)
        def _():
            q_wait(Q_UP0, k)
            q_dn(0, Q_UP0, Q_UP1, k).start()

    low = jnp.where(outer, T_L0 + 1, T_L0)
    q_near = jnp.where(outer, Q_UP1, Q_DN0)

    def q_relay(k):
        q_wait(q_near, k)

        @pl.when(outer)
        def _():
            q_dn(1, Q_UP1, Q_DN0, k).start()

        @pl.when(inner)
        def _():
            q_up(1, Q_DN0, Q_UP1, k).start()

        if k + 2 < CHUNKS:
            q_first(k + 2)
        tile = dot_nt(pb[P_OWN, k], qb[q_near, k])
        part[low] = tile if k == 0 else part[low] + tile

    active = [pair_ref[dp, level] > 0 for level in range(LEVELS)]
    x_active = pair_ref[partner_z(1) * per_z + xy, 2] > 0
    hit = (pos_ref[...] == lax.broadcasted_iota(jnp.int32, (rows, rows), 0)).astype(F32)

    def up_stats(level):
        finish_tile(T_U0 + level)
        tile = got[T_U0 + level]
        ms1[level] = jnp.broadcast_to(lse_cols(tile), (8, rows))
        m1_copy(level).start()
        return to_lanes(lse_rows(tile))

    def gather(parts):
        parts = [parts[0]] + [jnp.where(a, v, -jnp.inf) for a, v in zip(active, parts[1:])]
        top = functools.reduce(jnp.maximum, parts)
        return top + jnp.log(functools.reduce(jnp.add, [jnp.exp(v - top) for v in parts]))

    q_first(0)
    q_first(1)
    finish_tile(T_OWN)
    own_rows = lse_cols(got[T_OWN])
    own_cols = to_lanes(lse_rows(got[T_OWN]))
    row_parts = [own_rows, up_stats(0), up_stats(1)]
    q_relay(0)
    row_parts.append(up_stats(2))
    q_relay(1)
    q_relay(2)
    for level in range(LEVELS):
        m1_copy(level).wait_recv()
    row_lse = gather(row_parts)
    col_lse = gather([own_cols] + [mr1[level][0:1, :] for level in range(LEVELS)])
    ms2[0:4, :] = jnp.broadcast_to(row_lse, (4, rows))
    ms2[4:8, :] = jnp.broadcast_to(col_lse, (4, rows))
    for level in range(LEVELS):
        m2_copy(level).start()

    @pl.when(outer)
    def _():
        m2_copy(LEVELS).start()

    share = jnp.sum(row_lse) + jnp.sum(col_lse) - 2.0 * jnp.sum(got[T_OWN] * hit)
    lz[z] = jnp.full((8, 128), share, F32)
    for d in range(1, NZ):
        z_copy(d).start()
    q_relay(3)
    row_column = to_column(row_lse)
    col_column = to_column(col_lse)
    grad_t = jnp.exp(got[T_OWN] - row_lse) + jnp.exp(got[T_OWN] - col_column) - 2.0 * hit
    g_own_t[...] = grad_t.astype(BF16)
    g_own[...] = jnp.transpose(grad_t).astype(BF16)
    q_relay(4)
    q_relay(5)

    for level in range(LEVELS):
        m2_copy(level).wait_recv()

    def up_grad(level):
        tile = got[T_U0 + level]
        grad = jnp.exp(tile - row_column) + jnp.exp(tile - mr2[level][4:5, :])
        return jnp.where(active[level], grad, 0.0)

    @pl.when(inner)
    def _():
        m2_copy(LEVELS).wait_recv()
        finish_tile(T_X)
        tile = got[T_X]
        grad = jnp.exp(tile - mr2[LEVELS][0:1, :]) + jnp.exp(tile - to_column(mr2[1][4:5, :]))
        g_x[...] = jnp.where(x_active, grad, 0.0).astype(BF16)

    grad0 = up_grad(0)
    g_up[0] = grad0.astype(BF16)
    g_up0_t[...] = jnp.transpose(grad0).astype(BF16)
    q_relay(6)
    g_up[1] = up_grad(1).astype(BF16)
    q_relay(7)
    tile_copy(low).start()
    g_up[2] = up_grad(2).astype(BF16)

    @each_chunk
    def _(k):
        @pl.when(inner)
        def _():
            cs[k] = dot_nn(g_x[...], qb[Q_DN2, k]).astype(BF16)
            c_up(k).start()

        @pl.when(outer)
        def _():
            q_wait(Q_DN0, k)
            q_up(2, Q_DN0, Q_DN1, k).start()

    def low_grad(level):
        finish_tile(T_L0 + level)
        tile = got[T_L0 + level]
        grad = jnp.exp(tile - mr2[level][0:1, :]) + jnp.exp(tile - col_column)
        g_low[level] = jnp.where(active[level], grad, 0.0).astype(BF16)

    for d in range(1, NZ):
        z_wait(d)
    lx[x] = functools.reduce(jnp.add, [lz[i] for i in range(NZ)])
    for d in range(1, nx):
        x_copy(d).start()

    @each_chunk
    def _(k):
        @pl.when(inner)
        def _():
            remote(cs.at[k], cin.at[k], c_send.at[0, k], c_recv.at[k], up).wait_recv()
            cm[k] = (cin[k].astype(F32) + dot_nn(g_up0_t[...], qb[Q_OWN, k])).astype(BF16)
            c_dn(k).start()

        total = dot_nn(g_own[...], pb[P_OWN, k])
        total = total + dot_nn(g_up[0], pb[near, k])
        total = total + dot_nn(g_up[1], pb[P_UP1, k])
        total = total + dot_nn(g_up[2], pb[P_DN1, k])
        dqv[k] = total
        store_dq(k).start()

        @pl.when(inner)
        def _():
            q_wait(Q_UP1, k)
            add_tile(T_L0 + 1, k, pb[P_OWN, k], qb[Q_UP1, k])

    for d in range(1, nx):
        x_wait(d)
    ly[y] = functools.reduce(jnp.add, [lx[i] for i in range(nx)])
    for d in range(1, ny):
        y_copy(d).start()

    @pl.when(outer)
    def _():
        low_grad(1)

        @each_chunk
        def _(k):
            dpv[k] = dot_nn(g_own_t[...], qb[Q_OWN, k]) + dot_nn(g_low[1], qb[Q_UP1, k])

        @each_chunk
        def _(k):
            remote(cs.at[k], cin.at[k], c_send.at[0, k], c_recv.at[k], up).wait_recv()
            dpv[k] = dpv[k] + cin[k].astype(F32)
            store_dp(k).start()

    @pl.when(inner)
    def _():
        tile_copy(T_L0 + 1).start()
        low_grad(0)

        @each_chunk
        def _(k):
            q_wait(Q_DN1, k)
            add_tile(T_L0 + 2, k, pb[P_OWN, k], qb[Q_DN1, k])

        tile_copy(T_L0 + 2).start()
        low_grad(1)

        @each_chunk
        def _(k):
            total = dot_nn(g_own_t[...], qb[Q_OWN, k])
            total = total + dot_nn(g_low[0], qb[Q_DN0, k])
            dpv[k] = total + dot_nn(g_low[1], qb[Q_UP1, k])

        low_grad(2)

        @each_chunk
        def _(k):
            dpv[k] = dpv[k] + dot_nn(g_low[2], qb[Q_DN1, k])
            store_dp(k).start()

    for d in range(1, ny):
        y_wait(d)
    total_loss = functools.reduce(jnp.add, [ly[i] for i in range(ny)])
    loss_ref[0] = jnp.max(total_loss) / count

    @each_chunk
    def _(k):
        store_dq(k).wait()
        store_dp(k).wait()
        p_up(0, P_OWN, P_DN0, k).wait_send()
        p_up(1, P_DN0, P_DN1, k).wait_send()
        p_dn(0, P_UP1, P_DN0, k).wait_send()
        p_dn(1, P_UP2, P_DN1, k).wait_send()
        q_up(0, Q_DN2, Q_DN2, k).wait_send()
        q_up(1, Q_OWN, Q_DN0, k).wait_send()
        q_dn(0, Q_OWN, Q_DN2, k).wait_send()

        @pl.when(outer)
        def _():
            q_up(2, Q_DN0, Q_DN1, k).wait_send()
            q_dn(1, Q_UP1, Q_DN0, k).wait_send()

        @pl.when(inner)
        def _():
            p_dn(2, P_UP1, P_UP2, k).wait_send()
            c_up(k).wait_send()
            c_dn(k).wait_send()

    tile_copy(T_OWN).wait_send()
    for level in range(LEVELS):
        tile_copy(T_U0 + level).wait_send()
        m1_copy(level).wait_send()
        m2_copy(level).wait_send()
    tile_copy(T_L0 + 1).wait_send()

    @pl.when(outer)
    def _():
        m2_copy(LEVELS).wait_send()

    @pl.when(inner)
    def _():
        tile_copy(T_X).wait_send()
        tile_copy(T_L0).wait_send()
        tile_copy(T_L0 + 2).wait_send()

    for d in range(1, NZ):
        z_copy(d).wait_send()
    for d in range(1, nx):
        x_copy(d).wait_send()
    for d in range(1, ny):
        y_copy(d).wait_send()


def local(nx, ny, queries, passages, positive, pair_on):
    rows, depth = queries.shape
    width = depth // CHUNKS
    full = depth * lax.axis_size("sub")
    count = 2.0 * rows * lax.axis_size("dp")
    dma = pltpu.SemaphoreType.DMA
    block = (CHUNKS, rows, width)
    tile = (rows, rows)
    anywhere = pl.BlockSpec(memory_space=pl.ANY)
    return pl.pallas_call(
        functools.partial(kernel, nx, ny, 1.0 / math.sqrt(full), count),
        out_shape=(
            jax.ShapeDtypeStruct((1,), F32),
            jax.ShapeDtypeStruct((rows, depth), F32),
            jax.ShapeDtypeStruct((rows, depth), F32),
        ),
        in_specs=[
            anywhere,
            anywhere,
            pl.BlockSpec(memory_space=pltpu.VMEM),
            pl.BlockSpec(memory_space=pltpu.SMEM),
        ],
        out_specs=(pl.BlockSpec(memory_space=pltpu.SMEM), anywhere, anywhere),
        scratch_shapes=[
            pltpu.VMEM((6,) + block, BF16),
            pltpu.VMEM((6,) + block, BF16),
            pltpu.VMEM(block, BF16),
            pltpu.VMEM(block, BF16),
            pltpu.VMEM(block, BF16),
            pltpu.VMEM((8,) + tile, F32),
            pltpu.VMEM((8,) + tile, F32),
            pltpu.VMEM(block, F32),
            pltpu.VMEM(block, F32),
            pltpu.VMEM(tile, BF16),
            pltpu.VMEM(tile, BF16),
            pltpu.VMEM((LEVELS,) + tile, BF16),
            pltpu.VMEM(tile, BF16),
            pltpu.VMEM((LEVELS,) + tile, BF16),
            pltpu.VMEM(tile, BF16),
            pltpu.VMEM((LEVELS, 8, rows), F32),
            pltpu.VMEM((LEVELS, 8, rows), F32),
            pltpu.VMEM((8, rows), F32),
            pltpu.VMEM((LEVELS + 1, 8, rows), F32),
            pltpu.VMEM((NZ, 8, 128), F32),
            pltpu.VMEM((nx, 8, 128), F32),
            pltpu.VMEM((ny, 8, 128), F32),
            dma((2, CHUNKS)),
            dma((2, CHUNKS)),
            dma((2, CHUNKS)),
            dma((3, CHUNKS)),
            dma((5, CHUNKS)),
            dma((3, CHUNKS)),
            dma((2, CHUNKS)),
            dma((5, CHUNKS)),
            dma((2, CHUNKS)),
            dma((CHUNKS,)),
            dma((8,)),
            dma((8,)),
            dma((LEVELS,)),
            dma((LEVELS,)),
            dma((LEVELS + 1,)),
            dma((LEVELS + 1,)),
            dma((NZ,)),
            dma((NZ,)),
            dma((nx,)),
            dma((nx,)),
            dma((ny,)),
            dma((ny,)),
        ],
        compiler_params=pltpu.CompilerParams(
            collective_id=1, has_side_effects=True, vmem_limit_bytes=58 << 20
        ),
        name="infonce",
    )(queries, passages, positive, pair_on)


def solution(mesh):
    per_z = mesh.shape["dp"] // NZ
    nx = math.isqrt(per_z)
    ny = per_z // nx
    return jax.shard_map(
        functools.partial(local, nx, ny),
        mesh=mesh,
        in_specs=(P("dp", "sub"), P("dp", "sub"), P("dp", None), P()),
        out_specs=(P(), P("dp", "sub"), P("dp", "sub")),
        check_vma=False,
    )
```

time: 980 us -> 248 us (0.25)
  blocking collectives: 560 us -> 0 us
  waiting for transfers between devices: 300 us -> 0 us
  Pallas kernels: 0 us -> 235 us
  matrix products: 38.9 us -> 0 us
  other arithmetic: 28.7 us -> 0 us
  starting transfers between devices: 23.9 us -> 0 us
  between operations: 19.8 us -> 2.41 us
    psum x1 -> x0, blocking collectives: 560 us -> none  [local(): total = lax.psum(local_total, 'dp')]
    ppermute x12 -> x0, waiting for transfers between devices: 268 us -> none  [swapped(): return lax.ppermute(block, axis, route)]
    pallas_call x0 -> x1, Pallas kernels: none -> 235 us  [local(): pl.pallas_call(functools.partial(kernel, nx, ny, 1.0 / math.sqrt(full), c...]
    dot_general x12 -> x0, matrix products: 38.9 us -> none  [the longest x4 13.9 us: transposed_product(): lax.dot_general(grad, block, (((0,), (0,)), ((), ())), preferred_element_...]
    psum x1 -> x0, waiting for transfers between devices: 31.5 us -> none  [local(): summed = lax.psum(jnp.stack(partial_tiles), 'sub')]
    ppermute x12 -> x0, starting transfers between devices: 23.8 us -> none  [swapped(): return lax.ppermute(block, axis, route)]
    add x2 -> x0, other arithmetic: 14.9 us -> none  [the longest x1 8.09 us: local(): query_grad = query_grad + near_term]
  transfers between devices with their start and end apart: 13 -> 0, of which waited for: 7 -> 0; matrix products, arithmetic and copies ran while one was open for 4% -> 0% of each run, Pallas kernels for 0% -> 0%
where the time goes in v1:
time: 248 us; the launch traced here: 245 us
  Pallas kernels  235 us (95%)
  local copies, waits for them, and re-layouts  7.14 us (3%)
    pallas_call x1, Pallas kernels, local(): pl.pallas_call(functools.partial(kernel, nx, ny, 1.0 / math.sqrt(full), c...  235 us
    unnamed x5, local copies, waits for them, and re-layouts  7.14 us

profile of v1, /device:TPU:32, one launch (start us, length us, event | category | flops | bytes accessed | tf_op | source)
XLA Modules:
  0.0 244.6 jit_solution(16749396969178021380)
XLA Ops:
  0.6 1.4 copy.7.pair_ref
  2.0 235.1 %infonce.1 = (f32[1]{0:T(128)}, f32[384,2048]{1,0:T(8,128)}, f32[384,2048]{1,0:T(8,128)}) custom-call(bf16[384,2048]{1,0:T(8,128)(2,1)} %q_hbm.1, bf16[384,2048]{1,0:T(8,128)(2,1)} %p_hbm.1, s32[1,384]{1,0:T(1,128)} %pos_ref.1, s32[128,3]{1,0:T(8,128)} %copy.7.pair_ref), custom_call_target="tpu_custom_call" | custom-call | tf_op jit(solution)/shard_map/infonce/pallas_call | solution.py:576
  237.7 0.0 copy-start
  237.8 4.1 %copy.12 = f32[384,2048]{1,0:T(8,128)} copy(f32[384,2048]{1,0:T(8,128)} %get-tuple-element.7) | data formatting | bytes 6291456
  241.8 0.0 copy-done
  241.8 1.7 copy.13
Async XLA Ops:
  237.7 4.1 %copy-start = (f32[384,2048]{1,0:T(8,128)S(1)}, f32[384,2048]{1,0:T(8,128)}, u32[]{:S(2)}) copy-start(f32[384,2048]{1,0:T(8,128)} %get-tuple-element.8) | copy-start | bytes 9437188

commit v2 on v1

--- a/solution.py
+++ b/solution.py
@@ -12,6 +12,9 @@
 NZ = 8
 LEVELS = 3
 CHUNKS = 8
+LAG = 2
+EARLY = 2
+NEAR = 4
 F32 = jnp.float32
 BF16 = jnp.bfloat16
 
@@ -53,7 +56,7 @@
     q_hbm, p_hbm, pos_ref, pair_ref,
     loss_ref, dq_hbm, dp_hbm,
     pb, qb, cin, cs, cm, part, got, dqv, dpv,
-    g_own, g_own_t, g_up, g_up0_t, g_low, g_x,
+    g_own, g_own_t, g_up, g_up0_t, g_low, g_x, lse,
     ms1, mr1, ms2, mr2, lz, lx, ly,
     own_sem, out_sem,
     p_send_up, p_send_dn, p_recv,
@@ -190,6 +193,13 @@
 
         lax.fori_loop(0, CHUNKS, step, 0)
 
+    def each_step(body):
+        def step(k, carry):
+            body(k)
+            return carry
+
+        lax.fori_loop(0, CHUNKS + LAG, step, 0)
+
     def add_tile(i, k, left, right):
         @pl.when(k == 0)
         def _():
@@ -227,288 +237,359 @@
         @pl.when(inner)
         def _():
             p_up(0, P_OWN, P_UP0, k).start()
-            p_dn(0, P_OWN, P_UP0, k).start()
+
+            @pl.when(k < EARLY)
+            def _():
+                p_dn(0, P_OWN, P_UP0, k).start()
 
     @each_chunk
     def _(k):
         load_q(k).wait()
 
-        @pl.when(outer)
-        def _():
-            q_dn(0, Q_OWN, Q_DN2, k).start()
-
-    @each_chunk
-    def _(k):
+    near = jnp.where(outer, P_UP0, P_DN0)
+    active = [pair_ref[level, dp] > 0 for level in range(LEVELS)]
+    x_active = pair_ref[2, partner_z(1) * per_z + xy] > 0
+
+    def add_up(level, slot, k):
+        add_tile(T_U0 + level, k, qb[Q_OWN, k], pb[slot, k])
+
+    def add_low(level, slot, k):
+        add_tile(T_L0 + level, k, pb[P_OWN, k], qb[slot, k])
+
+    def add_own(k):
         add_tile(T_OWN, k, pb[P_OWN, k], qb[Q_OWN, k])
-
-    tile_copy(T_OWN).start()
-
-    near = jnp.where(outer, P_UP0, P_DN0)
-
-    @each_chunk
-    def _(k):
-        @pl.when(inner)
-        def _():
-            p_wait(P_UP0, k)
-            p_dn(1, P_UP0, P_UP1, k).start()
-
-        p_wait(near, k)
-
-        @pl.when(inner)
-        def _():
-            p_up(1, P_DN0, P_UP1, k).start()
-
-        add_tile(T_U0, k, qb[Q_OWN, k], pb[near, k])
-
-    tile_copy(T_U0).start()
-
-    @each_chunk
-    def _(k):
-        p_wait(P_UP1, k)
-
-        @pl.when(outer)
-        def _():
-            p_dn(0, P_UP1, P_DN0, k).start()
-
-        @pl.when(inner)
-        def _():
-            p_dn(2, P_UP1, P_UP2, k).start()
-
-        add_tile(T_U0 + 1, k, qb[Q_OWN, k], pb[P_UP1, k])
-
-        @pl.when(outer)
-        def _():
-            p_wait(P_DN0, k)
-            p_up(1, P_DN0, P_DN1, k).start()
-
-    tile_copy(T_U0 + 1).start()
-
-    @each_chunk
-    def _(k):
-        @pl.when(outer)
-        def _():
-            q_wait(Q_DN2, k)
-            q_up(0, Q_DN2, Q_DN2, k).start()
-
-        @pl.when(inner)
-        def _():
-            q_up(0, Q_OWN, Q_UP0, k).start()
-
-    @each_chunk
-    def _(k):
-        @pl.when(outer)
-        def _():
-            p_wait(P_UP2, k)
-            p_dn(1, P_UP2, P_DN1, k).start()
-
-        p_wait(P_DN1, k)
-        add_tile(T_U0 + 2, k, qb[Q_OWN, k], pb[P_DN1, k])
-
-        @pl.when(inner)
-        def _():
-            q_wait(Q_DN2, k)
-            add_tile(T_X, k, pb[P_UP1, k], qb[Q_DN2, k])
-
-    tile_copy(T_U0 + 2).start()
-
-    @pl.when(inner)
-    def _():
-        tile_copy(T_X).start()
-
-    def q_first(k):
-        @pl.when(outer)
-        def _():
-            q_up(1, Q_OWN, Q_DN0, k).start()
-
-        @pl.when(inner)
-        def _():
-            q_wait(Q_UP0, k)
-            q_dn(0, Q_UP0, Q_UP1, k).start()
-
-    low = jnp.where(outer, T_L0 + 1, T_L0)
-    q_near = jnp.where(outer, Q_UP1, Q_DN0)
-
-    def q_relay(k):
-        q_wait(q_near, k)
-
-        @pl.when(outer)
-        def _():
-            q_dn(1, Q_UP1, Q_DN0, k).start()
-
-        @pl.when(inner)
-        def _():
-            q_up(1, Q_DN0, Q_UP1, k).start()
-
-        if k + 2 < CHUNKS:
-            q_first(k + 2)
-        tile = dot_nt(pb[P_OWN, k], qb[q_near, k])
-        part[low] = tile if k == 0 else part[low] + tile
-
-    active = [pair_ref[dp, level] > 0 for level in range(LEVELS)]
-    x_active = pair_ref[partner_z(1) * per_z + xy, 2] > 0
-    hit = (pos_ref[...] == lax.broadcasted_iota(jnp.int32, (rows, rows), 0)).astype(F32)
 
     def up_stats(level):
         finish_tile(T_U0 + level)
         tile = got[T_U0 + level]
         ms1[level] = jnp.broadcast_to(lse_cols(tile), (8, rows))
         m1_copy(level).start()
-        return to_lanes(lse_rows(tile))
+        lse[2 + level:3 + level, :] = to_lanes(lse_rows(tile))
+
+    def own_stats():
+        finish_tile(T_OWN)
+        lse[0:1, :] = lse_cols(got[T_OWN])
+        lse[1:2, :] = to_lanes(lse_rows(got[T_OWN]))
 
     def gather(parts):
         parts = [parts[0]] + [jnp.where(a, v, -jnp.inf) for a, v in zip(active, parts[1:])]
         top = functools.reduce(jnp.maximum, parts)
         return top + jnp.log(functools.reduce(jnp.add, [jnp.exp(v - top) for v in parts]))
 
-    q_first(0)
-    q_first(1)
-    finish_tile(T_OWN)
-    own_rows = lse_cols(got[T_OWN])
-    own_cols = to_lanes(lse_rows(got[T_OWN]))
-    row_parts = [own_rows, up_stats(0), up_stats(1)]
-    q_relay(0)
-    row_parts.append(up_stats(2))
-    q_relay(1)
-    q_relay(2)
-    for level in range(LEVELS):
-        m1_copy(level).wait_recv()
-    row_lse = gather(row_parts)
-    col_lse = gather([own_cols] + [mr1[level][0:1, :] for level in range(LEVELS)])
-    ms2[0:4, :] = jnp.broadcast_to(row_lse, (4, rows))
-    ms2[4:8, :] = jnp.broadcast_to(col_lse, (4, rows))
-    for level in range(LEVELS):
-        m2_copy(level).start()
+    def all_stats():
+        for level in range(LEVELS):
+            m1_copy(level).wait_recv()
+        row_lse = gather([lse[0:1, :]] + [lse[2 + level:3 + level, :] for level in range(LEVELS)])
+        col_lse = gather([lse[1:2, :]] + [mr1[level][0:1, :] for level in range(LEVELS)])
+        lse[5:6, :] = row_lse
+        lse[6:7, :] = col_lse
+        ms2[0:4, :] = jnp.broadcast_to(row_lse, (4, rows))
+        ms2[4:8, :] = jnp.broadcast_to(col_lse, (4, rows))
+        for level in range(LEVELS):
+            m2_copy(level).start()
+
+    def hits():
+        return (pos_ref[...] == lax.broadcasted_iota(jnp.int32, (rows, rows), 0)).astype(F32)
+
+    def loss_start():
+        share = jnp.sum(lse[5:7, :]) - 2.0 * jnp.sum(got[T_OWN] * hits())
+        lz[z] = jnp.full((8, 128), share, F32)
+        for d in range(1, NZ):
+            z_copy(d).start()
+
+    def loss_x():
+        for d in range(1, NZ):
+            z_wait(d)
+        lx[x] = functools.reduce(jnp.add, [lz[i] for i in range(NZ)])
+        for d in range(1, nx):
+            x_copy(d).start()
+
+    def loss_y():
+        for d in range(1, nx):
+            x_wait(d)
+        ly[y] = functools.reduce(jnp.add, [lx[i] for i in range(nx)])
+        for d in range(1, ny):
+            y_copy(d).start()
+
+    def own_grads():
+        tile = got[T_OWN]
+        grad = jnp.exp(tile - lse[5:6, :]) + jnp.exp(tile - to_column(lse[6:7, :])) - 2.0 * hits()
+        g_own_t[...] = grad.astype(BF16)
+        g_own[...] = jnp.transpose(grad).astype(BF16)
+
+    def up_grad(level, also_t=False):
+        tile = got[T_U0 + level]
+        grad = jnp.exp(tile - to_column(lse[5:6, :])) + jnp.exp(tile - mr2[level][4:5, :])
+        grad = jnp.where(active[level], grad, 0.0)
+        g_up[level] = grad.astype(BF16)
+        if also_t:
+            g_up0_t[...] = jnp.transpose(grad).astype(BF16)
+
+    def low_grad(level):
+        finish_tile(T_L0 + level)
+        tile = got[T_L0 + level]
+        grad = jnp.exp(tile - mr2[level][0:1, :]) + jnp.exp(tile - to_column(lse[6:7, :]))
+        g_low[level] = jnp.where(active[level], grad, 0.0).astype(BF16)
+
+    def c_wait(k):
+        remote(cs.at[k], cin.at[k], c_send.at[0, k], c_recv.at[k], up).wait_recv()
+
+    def query_grad(k):
+        total = dot_nn(g_own[...], pb[P_OWN, k])
+        total = total + dot_nn(g_up[0], pb[near, k])
+        total = total + dot_nn(g_up[1], pb[P_UP1, k])
+        dqv[k] = total + dot_nn(g_up[2], pb[P_DN1, k])
+        store_dq(k).start()
+
+    def add_passage_grad(level, slot):
+        @each_chunk
+        def _(k):
+            dpv[k] = dpv[k] + dot_nn(g_low[level], qb[slot, k])
+
+    def q_far(k):
+        q_wait(Q_DN2, k)
+        q_up(0, Q_DN2, Q_DN2, k).start()
+
+    def at(k, step, body):
+        pl.when(k == step)(body)
 
     @pl.when(outer)
     def _():
+        for k in range(EARLY):
+            q_dn(0, Q_OWN, Q_DN2, k).start()
+
+        @each_step
+        def _(k):
+            @pl.when(k < CHUNKS)
+            def _():
+                p_wait(P_UP1, k)
+                p_dn(0, P_UP1, P_DN0, k).start()
+                add_up(1, P_UP1, k)
+
+            @pl.when(k >= LAG)
+            def _():
+                p_wait(P_DN0, k - LAG)
+                p_up(1, P_DN0, P_DN1, k - LAG).start()
+
+        tile_copy(T_U0 + 1).start()
+        for k in range(NEAR):
+            q_up(1, Q_OWN, Q_DN0, k).start()
+        for k in range(EARLY):
+            q_far(k)
+
+        @each_step
+        def _(k):
+            @pl.when(k < CHUNKS)
+            def _():
+                p_wait(P_UP2, k)
+                p_dn(1, P_UP2, P_DN1, k).start()
+                add_own(k)
+
+            @pl.when(k >= LAG)
+            def _():
+                p_wait(P_DN1, k - LAG)
+                add_up(2, P_DN1, k - LAG)
+
+            at(k, 2, lambda: up_stats(1))
+
+            @pl.when(k == CHUNKS - 1)
+            def _():
+                for j in range(EARLY, CHUNKS):
+                    q_dn(0, Q_OWN, Q_DN2, j).start()
+
+        tile_copy(T_OWN).start()
+        tile_copy(T_U0 + 2).start()
+        own_stats()
+        up_stats(2)
+
+        @each_chunk
+        def _(k):
+            p_wait(P_UP0, k)
+            add_up(0, P_UP0, k)
+
+            @pl.when(k >= EARLY + LAG)
+            def _():
+                q_far(k - LAG)
+
+        tile_copy(T_U0).start()
+        up_stats(0)
+        q_far(CHUNKS - LAG)
+        all_stats()
         m2_copy(LEVELS).start()
-
-    share = jnp.sum(row_lse) + jnp.sum(col_lse) - 2.0 * jnp.sum(got[T_OWN] * hit)
-    lz[z] = jnp.full((8, 128), share, F32)
-    for d in range(1, NZ):
-        z_copy(d).start()
-    q_relay(3)
-    row_column = to_column(row_lse)
-    col_column = to_column(col_lse)
-    grad_t = jnp.exp(got[T_OWN] - row_lse) + jnp.exp(got[T_OWN] - col_column) - 2.0 * hit
-    g_own_t[...] = grad_t.astype(BF16)
-    g_own[...] = jnp.transpose(grad_t).astype(BF16)
-    q_relay(4)
-    q_relay(5)
-
-    for level in range(LEVELS):
-        m2_copy(level).wait_recv()
-
-    def up_grad(level):
-        tile = got[T_U0 + level]
-        grad = jnp.exp(tile - row_column) + jnp.exp(tile - mr2[level][4:5, :])
-        return jnp.where(active[level], grad, 0.0)
+        for k in range(CHUNKS - LAG + 1, CHUNKS):
+            q_far(k)
+        for k in range(NEAR, CHUNKS):
+            q_up(1, Q_OWN, Q_DN0, k).start()
+
+        @each_step
+        def _(k):
+            @pl.when(k < CHUNKS)
+            def _():
+                q_wait(Q_UP1, k)
+                q_dn(1, Q_UP1, Q_DN0, k).start()
+                add_low(1, Q_UP1, k)
+
+            @pl.when(k >= LAG)
+            def _():
+                q_wait(Q_DN0, k - LAG)
+                q_up(2, Q_DN0, Q_DN1, k - LAG).start()
+
+            at(k, 2, loss_start)
+            at(k, 3, own_grads)
+
+        tile_copy(T_L0 + 1).start()
+        for level in range(LEVELS):
+            m2_copy(level).wait_recv()
+            up_grad(level)
+        low_grad(1)
+        loss_x()
+
+        @each_chunk
+        def _(k):
+            query_grad(k)
+            dpv[k] = dot_nn(g_own_t[...], qb[Q_OWN, k]) + dot_nn(g_low[1], qb[Q_UP1, k])
+
+        loss_y()
+
+        @each_chunk
+        def _(k):
+            c_wait(k)
+            dpv[k] = dpv[k] + cin[k].astype(F32)
+            store_dp(k).start()
 
     @pl.when(inner)
     def _():
+        @each_chunk
+        def _(k):
+            p_wait(P_UP0, k)
+            p_dn(1, P_UP0, P_UP1, k).start()
+            p_wait(P_DN0, k)
+            p_up(1, P_DN0, P_UP1, k).start()
+            add_up(0, P_DN0, k)
+
+        tile_copy(T_U0).start()
+
+        @each_chunk
+        def _(k):
+            q_up(0, Q_OWN, Q_UP0, k).start()
+
+        @each_chunk
+        def _(k):
+            p_wait(P_UP1, k)
+            p_dn(2, P_UP1, P_UP2, k).start()
+            add_up(1, P_UP1, k)
+
+        for k in range(EARLY, CHUNKS):
+            p_dn(0, P_OWN, P_UP0, k).start()
+        tile_copy(T_U0 + 1).start()
+
+        @each_chunk
+        def _(k):
+            add_own(k)
+            p_wait(P_DN1, k)
+            add_up(2, P_DN1, k)
+
+        tile_copy(T_OWN).start()
+        tile_copy(T_U0 + 2).start()
+        up_stats(0)
+        up_stats(1)
+        up_stats(2)
+        own_stats()
+
+        @each_chunk
+        def _(k):
+            q_wait(Q_UP0, k)
+            q_dn(0, Q_UP0, Q_UP1, k).start()
+
+            @pl.when(k < NEAR)
+            def _():
+                q_wait(Q_DN0, k)
+                q_up(1, Q_DN0, Q_UP1, k).start()
+                add_low(0, Q_DN0, k)
+
+        def add_x(k):
+            q_wait(Q_DN2, k)
+            add_tile(T_X, k, pb[P_UP1, k], qb[Q_DN2, k])
+
+        @each_chunk
+        def _(k):
+            add_x(k)
+            at(k, CHUNKS - 2, all_stats)
+
+        tile_copy(T_X).start()
+        loss_start()
+        finish_tile(T_X)
+        m2_copy(1).wait_recv()
         m2_copy(LEVELS).wait_recv()
-        finish_tile(T_X)
         tile = got[T_X]
         grad = jnp.exp(tile - mr2[LEVELS][0:1, :]) + jnp.exp(tile - to_column(mr2[1][4:5, :]))
         g_x[...] = jnp.where(x_active, grad, 0.0).astype(BF16)
 
-    grad0 = up_grad(0)
-    g_up[0] = grad0.astype(BF16)
-    g_up0_t[...] = jnp.transpose(grad0).astype(BF16)
-    q_relay(6)
-    g_up[1] = up_grad(1).astype(BF16)
-    q_relay(7)
-    tile_copy(low).start()
-    g_up[2] = up_grad(2).astype(BF16)
-
-    @each_chunk
-    def _(k):
-        @pl.when(inner)
-        def _():
+        @each_chunk
+        def _(k):
             cs[k] = dot_nn(g_x[...], qb[Q_DN2, k]).astype(BF16)
             c_up(k).start()
 
-        @pl.when(outer)
-        def _():
-            q_wait(Q_DN0, k)
-            q_up(2, Q_DN0, Q_DN1, k).start()
-
-    def low_grad(level):
-        finish_tile(T_L0 + level)
-        tile = got[T_L0 + level]
-        grad = jnp.exp(tile - mr2[level][0:1, :]) + jnp.exp(tile - col_column)
-        g_low[level] = jnp.where(active[level], grad, 0.0).astype(BF16)
-
-    for d in range(1, NZ):
-        z_wait(d)
-    lx[x] = functools.reduce(jnp.add, [lz[i] for i in range(NZ)])
-    for d in range(1, nx):
-        x_copy(d).start()
-
-    @each_chunk
-    def _(k):
-        @pl.when(inner)
-        def _():
-            remote(cs.at[k], cin.at[k], c_send.at[0, k], c_recv.at[k], up).wait_recv()
-            cm[k] = (cin[k].astype(F32) + dot_nn(g_up0_t[...], qb[Q_OWN, k])).astype(BF16)
-            c_dn(k).start()
-
-        total = dot_nn(g_own[...], pb[P_OWN, k])
-        total = total + dot_nn(g_up[0], pb[near, k])
-        total = total + dot_nn(g_up[1], pb[P_UP1, k])
-        total = total + dot_nn(g_up[2], pb[P_DN1, k])
-        dqv[k] = total
-        store_dq(k).start()
-
-        @pl.when(inner)
-        def _():
+        m2_copy(0).wait_recv()
+        up_grad(0, True)
+        up_grad(1)
+        m2_copy(2).wait_recv()
+        up_grad(2)
+        own_grads()
+
+        @each_step
+        def _(k):
+            @pl.when(k < CHUNKS)
+            def _():
+                c_wait(k)
+                cm[k] = (cin[k].astype(F32) + dot_nn(g_up0_t[...], qb[Q_OWN, k])).astype(BF16)
+                c_dn(k).start()
+
+            @pl.when(jnp.logical_and(k >= 1, k < 1 + CHUNKS - NEAR))
+            def _():
+                late = NEAR + k - 1
+                q_wait(Q_DN0, late)
+                q_up(1, Q_DN0, Q_UP1, late).start()
+                add_low(0, Q_DN0, late)
+
+            @pl.when(k < CHUNKS)
+            def _():
+                query_grad(k)
+                dpv[k] = dot_nn(g_own_t[...], qb[Q_OWN, k])
+
+            @pl.when(jnp.logical_and(k >= 2, k < 2 + NEAR))
+            def _():
+                q_wait(Q_UP1, k - 2)
+                add_low(1, Q_UP1, k - 2)
+
+            at(k, CHUNKS - NEAR + 1, lambda: tile_copy(T_L0).start())
+            at(k, CHUNKS - NEAR + 2, lambda: low_grad(0))
+
+        loss_x()
+
+        @each_chunk
+        def _(k):
+            q_wait(Q_DN1, k)
+            add_low(2, Q_DN1, k)
+
+        tile_copy(T_L0 + 2).start()
+        add_passage_grad(0, Q_DN0)
+        low_grad(2)
+        loss_y()
+        add_passage_grad(2, Q_DN1)
+
+        def rest(k, carry):
             q_wait(Q_UP1, k)
-            add_tile(T_L0 + 1, k, pb[P_OWN, k], qb[Q_UP1, k])
-
-    for d in range(1, nx):
-        x_wait(d)
-    ly[y] = functools.reduce(jnp.add, [lx[i] for i in range(nx)])
-    for d in range(1, ny):
-        y_copy(d).start()
-
-    @pl.when(outer)
-    def _():
+            add_low(1, Q_UP1, k)
+            return carry
+
+        lax.fori_loop(NEAR, CHUNKS, rest, 0)
+        tile_copy(T_L0 + 1).start()
         low_grad(1)
 
         @each_chunk
         def _(k):
-            dpv[k] = dot_nn(g_own_t[...], qb[Q_OWN, k]) + dot_nn(g_low[1], qb[Q_UP1, k])
-
-        @each_chunk
-        def _(k):
-            remote(cs.at[k], cin.at[k], c_send.at[0, k], c_recv.at[k], up).wait_recv()
-            dpv[k] = dpv[k] + cin[k].astype(F32)
-            store_dp(k).start()
-
-    @pl.when(inner)
-    def _():
-        tile_copy(T_L0 + 1).start()
-        low_grad(0)
-
-        @each_chunk
-        def _(k):
-            q_wait(Q_DN1, k)
-            add_tile(T_L0 + 2, k, pb[P_OWN, k], qb[Q_DN1, k])
-
-        tile_copy(T_L0 + 2).start()
-        low_grad(1)
-
-        @each_chunk
-        def _(k):
-            total = dot_nn(g_own_t[...], qb[Q_OWN, k])
-            total = total + dot_nn(g_low[0], qb[Q_DN0, k])
-            dpv[k] = total + dot_nn(g_low[1], qb[Q_UP1, k])
-
-        low_grad(2)
-
-        @each_chunk
-        def _(k):
-            dpv[k] = dpv[k] + dot_nn(g_low[2], qb[Q_DN1, k])
+            dpv[k] = dpv[k] + dot_nn(g_low[1], qb[Q_UP1, k])
             store_dp(k).start()
 
     for d in range(1, ny):
@@ -603,6 +684,7 @@
             pltpu.VMEM(tile, BF16),
             pltpu.VMEM((LEVELS,) + tile, BF16),
             pltpu.VMEM(tile, BF16),
+            pltpu.VMEM((8, rows), F32),
             pltpu.VMEM((LEVELS, 8, rows), F32),
             pltpu.VMEM((LEVELS, 8, rows), F32),
             pltpu.VMEM((8, rows), F32),
@@ -637,7 +719,7 @@
             collective_id=1, has_side_effects=True, vmem_limit_bytes=58 << 20
         ),
         name="infonce",
-    )(queries, passages, positive, pair_on)
+    )(queries, passages, positive, jnp.transpose(pair_on))
 
 
 def solution(mesh):

time: 248 us -> 203 us (0.82); the launches traced: 245 us -> 202 us
  Pallas kernels: 235 us -> 194 us
    pallas_call x1, Pallas kernels: 235 us -> 194 us  [local(): pl.pallas_call(functools.partial(kernel, nx, ny, 1.0 / math.sqrt(full), c...]
    unnamed x5 -> x4, local copies, waits for them, and re-layouts: 7.14 us -> 5.73 us
where the time goes in v2:
time: 203 us; the launch traced here: 202 us
  Pallas kernels  194 us (96%)
  local copies, waits for them, and re-layouts  5.73 us (3%)
  between operations  2.41 us (1%)
    pallas_call x1, Pallas kernels, local(): pl.pallas_call(functools.partial(kernel, nx, ny, 1.0 / math.sqrt(full), c...  194 us
    unnamed x4, local copies, waits for them, and re-layouts  5.73 us

profile of v2, /device:TPU:32, one launch (start us, length us, event | category | flops | bytes accessed | tf_op | source)
XLA Modules:
  0.0 202.4 jit_solution(8711866359717807673)
XLA Ops:
  0.6 194.3 %infonce.1 = (f32[1]{0:T(128)}, f32[384,2048]{1,0:T(8,128)}, f32[384,2048]{1,0:T(8,128)}) custom-call(bf16[384,2048]{1,0:T(8,128)(2,1)} %q_hbm.1, bf16[384,2048]{1,0:T(8,128)(2,1)} %p_hbm.1, s32[1,384]{1,0:T(1,128)} %pos_ref.1, s32[3,128]{1,0:T(4,128)} %bitcast.1), custom_call_target="tpu_custom_call" | custom-call | tf_op jit(solution)/shard_map/infonce/pallas_call | solution.py:657
  195.5 0.0 copy-start
  195.6 4.1 %copy.11 = f32[384,2048]{1,0:T(8,128)} copy(f32[384,2048]{1,0:T(8,128)} %get-tuple-element.7) | data formatting | bytes 6291456
  199.6 0.0 copy-done
  199.6 1.7 copy.12
Async XLA Ops:
  195.5 4.1 %copy-start = (f32[384,2048]{1,0:T(8,128)S(1)}, f32[384,2048]{1,0:T(8,128)}, u32[]{:S(2)}) copy-start(f32[384,2048]{1,0:T(8,128)} %get-tuple-element.8) | copy-start | bytes 9437188

commit v3 on v2

--- a/solution.py
+++ b/solution.py
@@ -13,7 +13,9 @@
 LEVELS = 3
 CHUNKS = 8
 LAG = 2
+SLOW = 3
 EARLY = 2
+FIRST = 3
 NEAR = 4
 F32 = jnp.float32
 BF16 = jnp.bfloat16
@@ -54,11 +56,11 @@
 def kernel(
     nx, ny, scale, count,
     q_hbm, p_hbm, pos_ref, pair_ref,
-    loss_ref, dq_hbm, dp_hbm,
+    loss_ref, dq_hbm, dp_hbm, block_hbm, grad_hbm,
     pb, qb, cin, cs, cm, part, got, dqv, dpv,
     g_own, g_own_t, g_up, g_up0_t, g_low, g_x, lse,
     ms1, mr1, ms2, mr2, lz, lx, ly,
-    own_sem, out_sem,
+    own_sem, out_sem, last_sem,
     p_send_up, p_send_dn, p_recv,
     q_send_up, q_send_dn, q_recv,
     c_send, c_recv,
@@ -186,6 +188,18 @@
             dpv.at[k], dp_hbm.at[:, pl.ds(pl.multiple_of(k * width, width), width)], out_sem.at[1, k]
         )
 
+    def store_block(k):
+        @pl.when(outer)
+        def _():
+            pltpu.make_async_copy(cin.at[k], block_hbm.at[k], last_sem.at[k]).start()
+
+        @pl.when(inner)
+        def _():
+            pltpu.make_async_copy(qb.at[Q_UP1, k], block_hbm.at[k], last_sem.at[k]).start()
+
+    def store_grad(i):
+        return pltpu.make_async_copy(g_low.at[i], grad_hbm, last_sem.at[CHUNKS])
+
     def each_chunk(body):
         def step(k, carry):
             body(k)
@@ -334,6 +348,35 @@
     def c_wait(k):
         remote(cs.at[k], cin.at[k], c_send.at[0, k], c_recv.at[k], up).wait_recv()
 
+    def settle():
+        @each_chunk
+        def _(k):
+            store_dq(k).wait()
+            p_up(0, P_OWN, P_DN0, k).wait_send()
+            p_up(1, P_DN0, P_DN1, k).wait_send()
+            p_dn(0, P_UP1, P_DN0, k).wait_send()
+            p_dn(1, P_UP2, P_DN1, k).wait_send()
+            q_up(0, Q_DN2, Q_DN2, k).wait_send()
+            q_dn(0, Q_OWN, Q_DN2, k).wait_send()
+
+        tile_copy(T_OWN).wait_send()
+        for level in range(LEVELS):
+            tile_copy(T_U0 + level).wait_send()
+            m1_copy(level).wait_send()
+            m2_copy(level).wait_send()
+        for d in range(1, NZ):
+            z_copy(d).wait_send()
+
+    def loss_end():
+        for d in range(1, ny):
+            y_wait(d)
+        total_loss = functools.reduce(jnp.add, [ly[i] for i in range(ny)])
+        loss_ref[0] = jnp.max(total_loss) / count
+        for d in range(1, nx):
+            x_copy(d).wait_send()
+        for d in range(1, ny):
+            y_copy(d).wait_send()
+
     def query_grad(k):
         total = dot_nn(g_own[...], pb[P_OWN, k])
         total = total + dot_nn(g_up[0], pb[near, k])
@@ -341,11 +384,6 @@
         dqv[k] = total + dot_nn(g_up[2], pb[P_DN1, k])
         store_dq(k).start()
 
-    def add_passage_grad(level, slot):
-        @each_chunk
-        def _(k):
-            dpv[k] = dpv[k] + dot_nn(g_low[level], qb[slot, k])
-
     def q_far(k):
         q_wait(Q_DN2, k)
         q_up(0, Q_DN2, Q_DN2, k).start()
@@ -355,7 +393,7 @@
 
     @pl.when(outer)
     def _():
-        for k in range(EARLY):
+        for k in range(FIRST):
             q_dn(0, Q_OWN, Q_DN2, k).start()
 
         @each_step
@@ -394,7 +432,7 @@
 
             @pl.when(k == CHUNKS - 1)
             def _():
-                for j in range(EARLY, CHUNKS):
+                for j in range(FIRST, CHUNKS):
                     q_dn(0, Q_OWN, Q_DN2, j).start()
 
         tile_copy(T_OWN).start()
@@ -448,14 +486,25 @@
         def _(k):
             query_grad(k)
             dpv[k] = dot_nn(g_own_t[...], qb[Q_OWN, k]) + dot_nn(g_low[1], qb[Q_UP1, k])
-
+            store_dp(k).start()
+
+        i = lax.broadcasted_iota(jnp.int32, (rows, rows), 0)
+        j = lax.broadcasted_iota(jnp.int32, (rows, rows), 1)
+        g_low[0] = (i == j).astype(F32).astype(BF16)
+        store_grad(0).start()
         loss_y()
+        settle()
+        loss_end()
+        m2_copy(LEVELS).wait_send()
+
+        @each_chunk
+        def _(k):
+            q_dn(1, Q_UP1, Q_DN0, k).wait_send()
 
         @each_chunk
         def _(k):
             c_wait(k)
-            dpv[k] = dpv[k] + cin[k].astype(F32)
-            store_dp(k).start()
+            store_block(k)
 
     @pl.when(inner)
     def _():
@@ -560,89 +609,135 @@
             @pl.when(jnp.logical_and(k >= 2, k < 2 + NEAR))
             def _():
                 q_wait(Q_UP1, k - 2)
+                store_block(k - 2)
                 add_low(1, Q_UP1, k - 2)
 
             at(k, CHUNKS - NEAR + 1, lambda: tile_copy(T_L0).start())
             at(k, CHUNKS - NEAR + 2, lambda: low_grad(0))
 
+            @pl.when(k >= SLOW)
+            def _():
+                q_wait(Q_DN1, k - SLOW)
+                add_low(2, Q_DN1, k - SLOW)
+
+        @each_chunk
+        def _(k):
+            dpv[k] = dpv[k] + dot_nn(g_low[0], qb[Q_DN0, k])
+
         loss_x()
 
-        @each_chunk
-        def _(k):
+        def rest_of_dn1(k, carry):
             q_wait(Q_DN1, k)
             add_low(2, Q_DN1, k)
-
+            return carry
+
+        lax.fori_loop(CHUNKS + LAG - SLOW, CHUNKS, rest_of_dn1, 0)
         tile_copy(T_L0 + 2).start()
-        add_passage_grad(0, Q_DN0)
-        low_grad(2)
-        loss_y()
-        add_passage_grad(2, Q_DN1)
-
-        def rest(k, carry):
+        settle()
+
+        @each_chunk
+        def _(k):
+            p_dn(2, P_UP1, P_UP2, k).wait_send()
+            c_up(k).wait_send()
+
+        def rest_of_up1(k, carry):
             q_wait(Q_UP1, k)
+            store_block(k)
             add_low(1, Q_UP1, k)
             return carry
 
-        lax.fori_loop(NEAR, CHUNKS, rest, 0)
+        lax.fori_loop(NEAR, CHUNKS - 2, rest_of_up1, 0)
+        loss_y()
+        low_grad(2)
+
+        @each_chunk
+        def _(k):
+            dpv[k] = dpv[k] + dot_nn(g_low[2], qb[Q_DN1, k])
+            store_dp(k).start()
+
+        lax.fori_loop(CHUNKS - 2, CHUNKS, rest_of_up1, 0)
         tile_copy(T_L0 + 1).start()
+        loss_end()
+        for i in (T_X, T_L0, T_L0 + 2):
+            tile_copy(i).wait_send()
         low_grad(1)
-
-        @each_chunk
-        def _(k):
-            dpv[k] = dpv[k] + dot_nn(g_low[1], qb[Q_UP1, k])
-            store_dp(k).start()
-
-    for d in range(1, ny):
-        y_wait(d)
-    total_loss = functools.reduce(jnp.add, [ly[i] for i in range(ny)])
-    loss_ref[0] = jnp.max(total_loss) / count
+        store_grad(1).start()
 
     @each_chunk
     def _(k):
-        store_dq(k).wait()
         store_dp(k).wait()
-        p_up(0, P_OWN, P_DN0, k).wait_send()
-        p_up(1, P_DN0, P_DN1, k).wait_send()
-        p_dn(0, P_UP1, P_DN0, k).wait_send()
-        p_dn(1, P_UP2, P_DN1, k).wait_send()
-        q_up(0, Q_DN2, Q_DN2, k).wait_send()
+        pltpu.make_async_copy(cin.at[k], block_hbm.at[k], last_sem.at[k]).wait()
         q_up(1, Q_OWN, Q_DN0, k).wait_send()
-        q_dn(0, Q_OWN, Q_DN2, k).wait_send()
 
         @pl.when(outer)
         def _():
             q_up(2, Q_DN0, Q_DN1, k).wait_send()
-            q_dn(1, Q_UP1, Q_DN0, k).wait_send()
 
         @pl.when(inner)
         def _():
-            p_dn(2, P_UP1, P_UP2, k).wait_send()
-            c_up(k).wait_send()
             c_dn(k).wait_send()
 
-    tile_copy(T_OWN).wait_send()
-    for level in range(LEVELS):
-        tile_copy(T_U0 + level).wait_send()
-        m1_copy(level).wait_send()
-        m2_copy(level).wait_send()
+    store_grad(0).wait()
     tile_copy(T_L0 + 1).wait_send()
 
-    @pl.when(outer)
-    def _():
-        m2_copy(LEVELS).wait_send()
-
-    @pl.when(inner)
-    def _():
-        tile_copy(T_X).wait_send()
-        tile_copy(T_L0).wait_send()
-        tile_copy(T_L0 + 2).wait_send()
-
-    for d in range(1, NZ):
-        z_copy(d).wait_send()
-    for d in range(1, nx):
-        x_copy(d).wait_send()
-    for d in range(1, ny):
-        y_copy(d).wait_send()
+
+def finish_kernel(dq, dp, blocks, grad, dq_out, dp_out, qv, pv, bv, gv, load, store):
+    width = blocks.shape[2]
+    rows = dq.shape[0] // CHUNKS
+
+    def columns(k):
+        return slice(k * width, (k + 1) * width)
+
+    def piece(k):
+        return slice(k * rows, (k + 1) * rows)
+
+    copy = pltpu.make_async_copy
+    loads = []
+    stores = []
+    first = copy(grad, gv, load.at[3, 0])
+    first.start()
+    for k in range(CHUNKS):
+        loads.append((
+            copy(dp.at[:, columns(k)], pv.at[:, columns(k)], load.at[0, k]),
+            copy(blocks.at[k], bv.at[k], load.at[1, k]),
+            copy(dq.at[piece(k)], qv.at[piece(k)], load.at[2, k]),
+        ))
+        for one in loads[-1]:
+            one.start()
+        stores.append((
+            copy(pv.at[:, columns(k)], dp_out.at[:, columns(k)], store.at[0, k]),
+            copy(qv.at[piece(k)], dq_out.at[piece(k)], store.at[1, k]),
+        ))
+    first.wait()
+    for k in range(CHUNKS):
+        for one in loads[k]:
+            one.wait()
+        stores[k][1].start()
+        pv[:, columns(k)] = pv[:, columns(k)] + dot_nn(gv[...], bv[k])
+        stores[k][0].start()
+    for k in range(CHUNKS):
+        for one in stores[k]:
+            one.wait()
+
+
+def finish(dq, dp, blocks, grad):
+    anywhere = pl.BlockSpec(memory_space=pl.ANY)
+    return pl.pallas_call(
+        finish_kernel,
+        out_shape=(jax.ShapeDtypeStruct(dq.shape, F32), jax.ShapeDtypeStruct(dp.shape, F32)),
+        in_specs=[anywhere] * 4,
+        out_specs=(anywhere, anywhere),
+        scratch_shapes=[
+            pltpu.VMEM(dq.shape, F32),
+            pltpu.VMEM(dp.shape, F32),
+            pltpu.VMEM(blocks.shape, BF16),
+            pltpu.VMEM(grad.shape, BF16),
+            pltpu.SemaphoreType.DMA((4, CHUNKS)),
+            pltpu.SemaphoreType.DMA((2, CHUNKS)),
+        ],
+        compiler_params=pltpu.CompilerParams(vmem_limit_bytes=60 << 20),
+        name="finish",
+    )(dq, dp, blocks, grad)
 
 
 def local(nx, ny, queries, passages, positive, pair_on):
@@ -654,12 +749,14 @@
     block = (CHUNKS, rows, width)
     tile = (rows, rows)
     anywhere = pl.BlockSpec(memory_space=pl.ANY)
-    return pl.pallas_call(
+    loss, dq, dp, last_block, last_grad = pl.pallas_call(
         functools.partial(kernel, nx, ny, 1.0 / math.sqrt(full), count),
         out_shape=(
             jax.ShapeDtypeStruct((1,), F32),
             jax.ShapeDtypeStruct((rows, depth), F32),
             jax.ShapeDtypeStruct((rows, depth), F32),
+            jax.ShapeDtypeStruct(block, BF16),
+            jax.ShapeDtypeStruct(tile, BF16),
         ),
         in_specs=[
             anywhere,
@@ -667,7 +764,7 @@
             pl.BlockSpec(memory_space=pltpu.VMEM),
             pl.BlockSpec(memory_space=pltpu.SMEM),
         ],
-        out_specs=(pl.BlockSpec(memory_space=pltpu.SMEM), anywhere, anywhere),
+        out_specs=(pl.BlockSpec(memory_space=pltpu.SMEM),) + (anywhere,) * 4,
         scratch_shapes=[
             pltpu.VMEM((6,) + block, BF16),
             pltpu.VMEM((6,) + block, BF16),
@@ -694,6 +791,7 @@
             pltpu.VMEM((ny, 8, 128), F32),
             dma((2, CHUNKS)),
             dma((2, CHUNKS)),
+            dma((CHUNKS + 1,)),
             dma((2, CHUNKS)),
             dma((3, CHUNKS)),
             dma((5, CHUNKS)),
@@ -720,6 +818,8 @@
         ),
         name="infonce",
     )(queries, passages, positive, jnp.transpose(pair_on))
+    dq, dp = finish(dq, dp, last_block, last_grad)
+    return loss, dq, dp
 
 
 def solution(mesh):

time: 203 us -> 203 us (level)
  Pallas kernels: 194 us -> 200 us
  local copies, waits for them, and re-layouts: 5.73 us -> 0 us
    pallas_call x0 -> x1, Pallas kernels: none -> 6.34 us  [finish(): pl.pallas_call(finish_kernel, out_shape=(jax.ShapeDtypeStruct(dq.shape, F...]
    unnamed x4 -> x0, local copies, waits for them, and re-layouts: 5.73 us -> none
where the time goes in v3:
time: 203 us; the launch traced here: 202 us
  Pallas kernels  200 us (99%)
  between operations  2.39 us (1%)
    pallas_call x1, Pallas kernels, local(): pl.pallas_call(functools.partial(kernel, nx, ny, 1.0 / math.sqrt(full), c...  194 us
    pallas_call x1, Pallas kernels, finish(): pl.pallas_call(finish_kernel, out_shape=(jax.ShapeDtypeStruct(dq.shape, F...  6.34 us

profile of v3, /device:TPU:32, one launch (start us, length us, event | category | flops | bytes accessed | tf_op | source)
XLA Modules:
  0.0 202.4 jit_solution(4824637259413317844)
XLA Ops:
  0.6 193.6 %infonce.1 = (f32[1]{0:T(128)}, f32[384,2048]{1,0:T(8,128)}, f32[384,2048]{1,0:T(8,128)}, bf16[8,384,256]{2,1,0:T(8,128)(2,1)}, bf16[384,384]{1,0:T(8,128)(2,1)}) custom-call(bf16[384,2048]{1,0:T(8,128)(2,1)} %q_hbm.1, bf16[384,2048]{1,0:T(8,128)(2,1)} %p_hbm.1, s32[1,384]{1,0:T(1,128)} %pos_ref.1, s32[3,128]{1,0:T(4,128)} %bitcast.1), custom_call_target="tpu_custom_call" | custom-call | tf_op jit(solution)/shard_map/infonce/pallas_call | solution.py:752
  194.3 6.3 %finish.1 = (f32[384,2048]{1,0:T(8,128)}, f32[384,2048]{1,0:T(8,128)}) custom-call(f32[384,2048]{1,0:T(8,128)} %get-tuple-element.11.dq, f32[384,2048]{1,0:T(8,128)} %get-tuple-element.12.dp, bf16[8,384,256]{2,1,0:T(8,128)(2,1)} %get-tuple-element.13.blocks, bf16[384,384]{1,0:T(8,128)(2,1)} %get-tuple-element.14.grad), custom_call_target="tpu_custom_call" | custom-call | tf_op jit(solution)/shard_map/finish/pallas_call | solution.py:725

commit v4 on v3

--- a/solution.py
+++ b/solution.py
@@ -223,14 +223,6 @@
         def _():
             part[i] = part[i] + dot_nt(left, right)
 
-    @each_chunk
-    def _(k):
-        load_p(k).start()
-
-    @each_chunk
-    def _(k):
-        load_q(k).start()
-
     barrier = pltpu.get_barrier_semaphore()
     greeted = [twin]
     greeted += [at_z(z + d) for d in range(1, NZ)]
@@ -238,6 +230,15 @@
     greeted += [y_device(d) for d in range(1, ny)]
     for device in greeted:
         pl.semaphore_signal(barrier, inc=1, device_id=device, device_id_type=MESH)
+
+    @each_chunk
+    def _(k):
+        load_p(k).start()
+
+    @each_chunk
+    def _(k):
+        load_q(k).start()
+
     pl.semaphore_wait(barrier, len(greeted))
 
     @each_chunk
@@ -564,9 +565,9 @@
         def _(k):
             add_x(k)
             at(k, CHUNKS - 2, all_stats)
+            at(k, CHUNKS - 2, loss_start)
 
         tile_copy(T_X).start()
-        loss_start()
         finish_tile(T_X)
         m2_copy(1).wait_recv()
         m2_copy(LEVELS).wait_recv()

time: 203 us -> 203 us (level)
  no operation moved by 1% of the time
where the time goes in v4:
time: 203 us; the launch traced here: 202 us
  Pallas kernels  200 us (99%)
  between operations  2.39 us (1%)
    pallas_call x1, Pallas kernels, local(): pl.pallas_call(functools.partial(kernel, nx, ny, 1.0 / math.sqrt(full), c...  193 us
    pallas_call x1, Pallas kernels, finish(): pl.pallas_call(finish_kernel, out_shape=(jax.ShapeDtypeStruct(dq.shape, F...  6.34 us

profile of v4, /device:TPU:32, one launch (start us, length us, event | category | flops | bytes accessed | tf_op | source)
XLA Modules:
  0.0 202.2 jit_solution(6062945996542430299)
XLA Ops:
  0.6 193.5 %infonce.1 = (f32[1]{0:T(128)}, f32[384,2048]{1,0:T(8,128)}, f32[384,2048]{1,0:T(8,128)}, bf16[8,384,256]{2,1,0:T(8,128)(2,1)}, bf16[384,384]{1,0:T(8,128)(2,1)}) custom-call(bf16[384,2048]{1,0:T(8,128)(2,1)} %q_hbm.1, bf16[384,2048]{1,0:T(8,128)(2,1)} %p_hbm.1, s32[1,384]{1,0:T(1,128)} %pos_ref.1, s32[3,128]{1,0:T(4,128)} %bitcast.1), custom_call_target="tpu_custom_call" | custom-call | tf_op jit(solution)/shard_map/infonce/pallas_call | solution.py:753
  194.1 6.3 %finish.1 = (f32[384,2048]{1,0:T(8,128)}, f32[384,2048]{1,0:T(8,128)}) custom-call(f32[384,2048]{1,0:T(8,128)} %get-tuple-element.11.dq, f32[384,2048]{1,0:T(8,128)} %get-tuple-element.12.dp, bf16[8,384,256]{2,1,0:T(8,128)(2,1)} %get-tuple-element.13.blocks, bf16[384,384]{1,0:T(8,128)(2,1)} %get-tuple-element.14.grad), custom_call_target="tpu_custom_call" | custom-call | tf_op jit(solution)/shard_map/finish/pallas_call | solution.py:726
